TPU v7x, 1024 devices: a whole 8x8x8 slice. The times are simulated.
1024 devices in a mesh: expert: 16 (over z, y_lo), tensor: 64 (over x, y_hi, core).
Axes of the slice: x: 8, y: 8 (y_hi: 4, y_lo: 2; y = y_hi * 2 + y_lo), z: 8, core: 2. Of those that a mesh axis runs over, the one named last changes fastest.
Arguments:
- tokens: bfloat16 [6144, 2048], P('expert', 'tensor'), may hold values from -6 to 6
- cotangent: bfloat16 [6144, 2048], P('expert', 'tensor'), may hold values from -6 to 6
- routing: int32 [16, 384], P('expert'), may hold values from 0 to 383, each once within a row
- up_weight: bfloat16 [32, 2048, 4096], P('expert', None, 'tensor'), may hold values from -0.125 to 0.125
- down_weight: bfloat16 [32, 4096, 2048], P('expert', 'tensor'), may hold values from -0.09375 to 0.09375
- expert_embed: bfloat16 [32, 2048], P('expert'), may hold values from -0.125 to 0.125
Outputs:
- tokens_grad: bfloat16 [6144, 2048], P('expert', 'tensor')
- up_grad: bfloat16 [32, 2048, 4096], P('expert', None, 'tensor')
- down_grad: bfloat16 [32, 4096, 2048], P('expert', 'tensor')
- embed_grad: float32 [32, 2048], P('expert', 'tensor')
Inputs may be any that keep to these rules, and one draw needn't show every extreme that they name: Each row of routing is a permutation of 0 .. 383; the entries at positions e * 12 .. (e + 1) * 12 - 1 are the tokens that this group assigns to expert e.
All inputs are finite; a program needn't handle non-finite values.
Results may differ from a plain program's by a relative error of at most 0.0075.
Values may be sent and summed in bfloat16 or wider, within the bound.
A program may use at most 32 MiB of HBM per device.

v0:
```python
import jax
import jax.numpy as jnp
from jax import lax
from jax.sharding import PartitionSpec as P


def local(tokens, cotangent, routing, up_weight, down_weight, expert_embed):
    tok_dev, col_width = tokens.shape
    groups = lax.axis_size("expert")
    local_experts = up_weight.shape[0]
    slot_rows = tok_dev // (groups * local_experts)
    expert_rows = groups * slot_rows
    offset = lax.axis_index("tensor") * col_width
    permuted = routing[0]
    sorted_x = jnp.take(tokens, permuted, axis=0).reshape(
        groups, local_experts * slot_rows, col_width
    )
    sorted_g = jnp.take(cotangent, permuted, axis=0).reshape(
        groups, local_experts * slot_rows, col_width
    )
    share_x, share_g = (
        lax.all_to_all(sorted_x, "expert", split_axis=0, concat_axis=0, tiled=True),
        lax.all_to_all(sorted_g, "expert", split_axis=0, concat_axis=0, tiled=True),
    )

    def regroup(share):
        share = share.reshape(groups, local_experts, slot_rows, col_width).transpose(1, 0, 2, 3)
        return share.reshape(local_experts, expert_rows, col_width)

    share_x = regroup(share_x)
    share_g = regroup(share_g)
    inputs, upstream = (
        lax.all_gather(share_x, "tensor", axis=2, tiled=True),
        lax.all_gather(share_g, "tensor", axis=2, tiled=True),
    )
    logits = jnp.einsum("erd,ed->er", inputs, expert_embed, preferred_element_type=jnp.float32)
    hidden = jnp.einsum("erd,edf->erf", inputs, up_weight, preferred_element_type=jnp.float32)
    back_raw = jnp.einsum("erd,efd->erf", upstream, down_weight, preferred_element_type=jnp.float32)
    gating = jax.nn.sigmoid(logits)
    activated, pullback = jax.vjp(jax.nn.gelu, hidden)
    activated = activated.astype(jnp.bfloat16)
    gate_part = jnp.sum(activated.astype(jnp.float32) * back_raw, axis=2)
    scaled = (gating[..., None] * upstream.astype(jnp.float32)).astype(jnp.bfloat16)
    down_grad = jnp.einsum(
        "erf,erd->efd", activated, scaled, preferred_element_type=jnp.float32
    ).astype(jnp.bfloat16)
    (pre_grad,) = pullback(gating[..., None] * back_raw)
    pre_grad = pre_grad.astype(jnp.bfloat16)
    up_grad = jnp.einsum(
        "erd,erf->edf", inputs, pre_grad, preferred_element_type=jnp.float32
    ).astype(jnp.bfloat16)
    hidden_terms = jnp.einsum(
        "erf,edf->erd", pre_grad, up_weight, preferred_element_type=jnp.float32
    )
    gate_total = lax.psum(gate_part, "tensor")
    summed = lax.psum_scatter(hidden_terms, "tensor", scatter_dimension=2, tiled=True)
    slopes = gate_total * gating * (1.0 - gating)
    emb_cols = lax.dynamic_slice_in_dim(expert_embed, offset, col_width, 1).astype(jnp.float32)
    summed = (summed + slopes[..., None] * emb_cols[:, None, :]).astype(jnp.bfloat16)
    outgoing = summed.reshape(local_experts, groups, slot_rows, col_width).transpose(1, 0, 2, 3)
    outgoing = outgoing.reshape(groups, local_experts * slot_rows, col_width)
    returned = lax.all_to_all(outgoing, "expert", split_axis=0, concat_axis=0, tiled=True).reshape(
        tok_dev, col_width
    )
    placed = jnp.zeros((tok_dev, col_width), jnp.bfloat16).at[permuted].set(returned)
    token_grad = (cotangent.astype(jnp.float32) + placed.astype(jnp.float32)).astype(jnp.bfloat16)
    emb_grad = jnp.sum(slopes[..., None] * share_x.astype(jnp.float32), axis=1)
    return (token_grad, up_grad, down_grad, emb_grad)


def solution(mesh):
    return jax.shard_map(
        local,
        mesh=mesh,
        in_specs=(
            P("expert", "tensor"),
            P("expert", "tensor"),
            P("expert", None),
            P("expert", None, "tensor"),
            P("expert", "tensor", None),
            P("expert", None),
        ),
        out_specs=(
            P("expert", "tensor"),
            P("expert", None, "tensor"),
            P("expert", "tensor", None),
            P("expert", "tensor"),
        ),
        check_vma=False,
    )
```

profile of v0, /device:TPU:1, one launch (start us, length us, event | category | flops | bytes accessed | tf_op | source)
XLA Modules:
  0.0 547.7 jit_solution(18304379599838386000)
XLA Ops:
  7.2 0.7 reduce.2
  8.0 0.9 copy.29
  8.9 0.9 copy.30
  9.7 1.4 gather_fusion.1
  11.2 1.4 gather_fusion
  12.9 25.7 %all_to_all.15 = bf16[16,2,384]{2,1,0:T(2,128)(2,1)S(1)} all-to-all(bf16[16,2,384]{2,1,0:T(2,128)(2,1)S(1)} %reshape.117), channel_id=1, replica_groups=mesh['expert'=16,'tensor'=64] {'expert'}, dimensions={0} | all-to-all | bytes 49152 | tf_op jit(solution)/shard_map/all_to_all | solution.py:22
  38.9 0.7 copy.33
  39.8 10.0 %all_to_all.16 = bf16[16,2,384]{2,1,0:T(2,128)(2,1)S(1)} all-to-all(bf16[16,2,384]{2,1,0:T(2,128)(2,1)S(1)} %reshape.119), channel_id=1, replica_groups=mesh['expert'=16,'tensor'=64] {'expert'}, dimensions={0} | all-to-all | bytes 49152 | tf_op jit(solution)/shard_map/all_to_all | solution.py:23
  50.0 0.7 copy.37
  50.8 76.3 %all-gather.3.cloned.1.call-done = bf16[2,192,2048]{1,2,0:T(8,128)(2,1)} async-done(((bf16[2,192,32]{1,2,0:T(8,128)(2,1)}), bf16[2,192,2048]{1,2,0:T(8,128)(2,1)}) %all-gather.3.cloned.1.call-update) | async-done | bytes 1572880 | tf_op jit(solution)/shard_map/all_gather | solution.py:33
  127.1 2.1 fusion.18
  129.1 90.7 %all-gather.5.cloned.1.call-done = bf16[2,192,2048]{1,2,0:T(8,128)(2,1)} async-done(((bf16[2,192,32]{1,2,0:T(8,128)(2,1)}), bf16[2,192,2048]{1,2,0:T(8,128)(2,1)}) %all-gather.5.cloned.1.call-update) | async-done | bytes 1572880 | tf_op jit(solution)/shard_map/all_gather | solution.py:34
  219.8 2.7 multiply_reduce_fusion.1
  222.5 138.7 %psum.7 = f32[2,192]{1,0:T(2,128)S(1)} all-reduce(f32[2,192]{1,0:T(2,128)S(1)} %get-tuple-element.17), channel_id=1, replica_groups=mesh['expert'=16,'tensor'=64] {'tensor'}, use_global_device_ids=true, to_apply=%region_2.4 | all-reduce | flops 384 | bytes 3072 | tf_op jit(solution)/shard_map/psum | solution.py:55
  361.7 2.7 fusion.17
  365.3 1.6 convolution_convert_fusion.1
  366.9 1.6 convolution_convert_fusion
  368.4 153.1 %reduce-scatter.2.cloned.1.call-done = f32[2,192,32]{1,2,0:T(8,128)} async-done(((f32[2,192,2048]{1,2,0:T(8,128)}), f32[2,192,32]{1,2,0:T(8,128)}) %reduce-scatter.2.cloned.1.call-update) | async-done | bytes 49168 | tf_op jit(solution)/shard_map/reduce_scatter | solution.py:56
  521.5 0.9 add_convert_fusion.1
  522.6 0.7 reshape.121
  523.4 8.0 %all-to-all-start.2 = ((bf16[16,2,384]{2,1,0:T(2,128)(2,1)}), bf16[16,2,384]{2,1,0:T(2,128)(2,1)S(1)}, u32[]{:S(2)}, u32[]{:S(2)}) async-start(bf16[16,2,384]{2,1,0:T(2,128)(2,1)} %reshape.121), calls=%async_computation.3 | async-start | bytes 49152 | tf_op jit(solution)/shard_map/all_to_all | solution.py:62
  531.3 0.7 multiply_reduce_fusion
  532.0 6.7 %all-to-all-done.2 = bf16[16,2,384]{2,1,0:T(2,128)(2,1)S(1)} async-done(((bf16[16,2,384]{2,1,0:T(2,128)(2,1)}), bf16[16,2,384]{2,1,0:T(2,128)(2,1)S(1)}, u32[]{:S(2)}, u32[]{:S(2)}) %all-to-all-start.2) | async-done | bytes 24608 | tf_op jit(solution)/shard_map/all_to_all | solution.py:62
  538.9 1.5 scatter_custom_fusion
  (45 shorter events, 3.4 us)
Async XLA Ops:
  7.2 119.9 %copy-start = (bf16[2,2048,64]{1,2,0:T(8,128)(2,1)S(1)}, bf16[2,2048,64]{1,2,0:T(8,128)(2,1)}, u32[]{:S(2)}) copy-start(bf16[2,2048,64]{1,2,0:T(8,128)(2,1)} %param.11) | copy-start | bytes 1572868
  7.2 119.9 %all-gather.3.cloned.1.call-start = ((), (), s32[]{:S(2)}) async-start(), calls=%async_computation.4 | async-start | bytes 2129920 | tf_op jit(solution)/shard_map/all_gather | solution.py:33
  38.7 181.1 %copy-start.3 = (bf16[2,64,2048]{2,1,0:T(8,128)(2,1)S(1)}, bf16[2,64,2048]{2,1,0:T(8,128)(2,1)}, u32[]{:S(2)}) copy-start(bf16[2,64,2048]{2,1,0:T(8,128)(2,1)} %param.12) | copy-start | bytes 1572868
  39.6 180.2 %all-gather.5.cloned.1.call-start = ((), (), s32[]{:S(2)}) async-start(), calls=%async_computation.5 | async-start | bytes 2129920 | tf_op jit(solution)/shard_map/all_gather | solution.py:34
  50.7 470.8 %reduce-scatter.2.cloned.1.call-start = ((), (), s32[]{:S(2)}) async-start(), calls=%async_computation.6 | async-start | bytes 4259840 | tf_op jit(solution)/shard_map/reduce_scatter | solution.py:56
  129.1 232.1 %copy-start.1 = (bf16[2,192,2048]{1,2,0:T(8,128)(2,1)S(1)}, bf16[2,192,2048]{1,2,0:T(8,128)(2,1)}, u32[]{:S(2)}) copy-start(bf16[2,192,2048]{1,2,0:T(8,128)(2,1)} %all-gather.3.cloned.1.call-done) | copy-start | bytes 4718596
  129.1 232.1 %copy-start.5 = (bf16[2,2048]{1,0:T(2,128)(2,1)S(1)}, bf16[2,2048]{1,0:T(2,128)(2,1)}, u32[]{:S(2)}) copy-start(bf16[2,2048]{1,0:T(2,128)(2,1)} %param.13) | copy-start | bytes 24580
  222.5 139.1 %copy-start.4 = (f32[2,192,64]{1,2,0:T(8,128)S(1)}, f32[2,192,64]{1,2,0:T(8,128)}, u32[]{:S(2)}) copy-start(f32[2,192,64]{1,2,0:T(8,128)} %get-tuple-element.18) | copy-start | bytes 294916
  364.4 0.7 copy-start.6
  365.3 1.6 copy-start.2
  523.4 15.4 %all-to-all-start.2 = ((bf16[16,2,384]{2,1,0:T(2,128)(2,1)}), bf16[16,2,384]{2,1,0:T(2,128)(2,1)S(1)}, u32[]{:S(2)}, u32[]{:S(2)}) async-start(bf16[16,2,384]{2,1,0:T(2,128)(2,1)} %reshape.121), calls=%async_computation.3 | async-start | bytes 49152 | tf_op jit(solution)/shard_map/all_to_all | solution.py:62
Sparse Core Ops, SparseCore 0:
  39.7 87.2 all-gather.2
  132.1 87.6 all-gather.4
  364.6 156.9 reduce-scatter.1
where the time goes:
time: 553 us; the launch traced here: 548 us
  waiting for transfers between devices  327 us (59%)
  blocking collectives  174 us (31%)
  between operations  14 us (3%)
  matrix products  11 us (2%)
  local copies, waits for them, and re-layouts  10.7 us (2%)
  starting transfers between devices  8.11 us (1%)
    reduce_scatter x1, waiting for transfers between devices, local(): lax.psum_scatter(hidden_terms, 'tensor', scatter_dimension=2, tiled=True)  153 us
    psum x1, blocking collectives, local(): gate_total = lax.psum(gate_part, 'tensor')  139 us
    all_gather x1, waiting for transfers between devices, local(): lax.all_gather(share_g, 'tensor', axis=2, tiled=True)  90.7 us
    all_gather x1, waiting for transfers between devices, local(): lax.all_gather(share_x, 'tensor', axis=2, tiled=True)  76.3 us
    all_to_all x1, blocking collectives, local(): lax.all_to_all(sorted_x, 'expert', split_axis=0, concat_axis=0, tiled=True)  25.7 us
  transfers between devices with their start and end apart: 4, of which 4 were waited for; matrix products, arithmetic and copies ran while one was open for 1% of the time, Pallas kernels for 0%

commit v1 on v0

v1 whole, which is shorter than its diff:
```python
import functools

import jax
import jax.numpy as jnp
from jax import lax
from jax.experimental import pallas as pl
from jax.experimental.pallas import tpu as pltpu
from jax.sharding import PartitionSpec as P

Y = 4
KP = 16
BF = jnp.bfloat16
F32 = jnp.float32
NN = ((1,), (0,))
NT = ((1,), (1,))
TN = ((0,), (0,))


def dot(a, b, dims):
    return lax.dot_general(a, b, (dims, ((), ())), preferred_element_type=F32)


def remote(src, dst, ssem, rsem, device):
    return pltpu.make_async_remote_copy(
        src_ref=src,
        dst_ref=dst,
        send_sem=ssem,
        recv_sem=rsem,
        device_id=device,
        device_id_type=pl.DeviceIdType.MESH,
    )


def ones_where(hit):
    return hit.astype(F32).astype(BF)


def kernel(
    dims,
    tok_hbm, cot_hbm, rt_hbm, up_hbm, down_hbm, emb_hbm,
    tg_hbm, ug_hbm, dg_hbm, eg_hbm,
    both, rt, emb, ot, otq, bh, sbuf, rbuf, xg, w, u2, acc, l2, bd, gr,
    pf, outb, inb, vf, yo, yi, gp, gy, gs, gx, ego, egi, egv, tgv, sbuf2, rbuf2,
    lsem, osem,
    w_s, w_r, a_s, a_r, y_s, y_r, ring_s, ring_r, ch_s, ch_r, yr_s, yr_r,
    gy_s, gy_r, gx_s, gx_r, g_s, g_r, e_s, e_r, b_s, b_r,
):
    NE, SL, CW, X, FL = dims
    H = X // 2
    HR = NE * SL
    R = 2 * HR
    NQ = NE * KP
    CF = 2 * FL
    SW = Y * 2 * CW
    CH = 2 * CW
    PW = Y * CW
    D = X * SW
    e = lax.axis_index("expert")
    t = lax.axis_index("tensor")
    core = lax.rem(t, 2)
    chip = t // 2
    y = lax.rem(chip, Y)
    x = chip // Y
    other = 1 - core

    def xa(d):
        return lax.rem(x + (d + X), X)

    def ya(d):
        return lax.rem(y + (d + Y), Y)

    def ea(d):
        return lax.rem(e + (d + NE), NE)

    def tid(xx, yy, cc):
        return (xx * Y + yy) * 2 + cc

    sib = (e, tid(x, y, other))
    sends = []

    def go(src, dst, ssem, rsem, device):
        copy = remote(src, dst, ssem, rsem, device)
        copy.start()
        sends.append(copy)

    def drain():
        for copy in sends:
            copy.wait_send()
        sends.clear()

    def got(dst, ssem, rsem):
        remote(dst, dst, ssem, rsem, sib).wait_recv()

    barrier = pltpu.get_barrier_semaphore()
    pairs = [(rel, o) for o in range(NE) for rel in range(2) if rel or o]
    peers = [(ea(o), tid(x, y, core if rel == 0 else other)) for rel, o in pairs]
    peers += [(e, tid(x, ya(dy), core)) for dy in range(1, Y)]
    peers += [(e, tid(xa(dx), y, core)) for dx in range(1, X)]
    for peer in peers:
        pl.semaphore_signal(barrier, inc=1, device_id=peer, device_id_type=pl.DeviceIdType.MESH)

    loads = [
        pltpu.make_async_copy(rt_hbm, rt, lsem.at[0]),
        pltpu.make_async_copy(tok_hbm, both.at[pl.ds(0, CW)], lsem.at[1]),
        pltpu.make_async_copy(cot_hbm, both.at[pl.ds(CW, CW)], lsem.at[2]),
        pltpu.make_async_copy(emb_hbm, emb, lsem.at[3]),
        pltpu.make_async_copy(
            up_hbm.at[pl.ds(pl.multiple_of(core * FL, FL), FL)],
            w.at[pl.ds(pl.multiple_of(core * FL, FL), FL)],
            lsem.at[4],
        ),
        pltpu.make_async_copy(
            down_hbm.at[pl.ds(pl.multiple_of(core * FL, FL), FL)],
            w.at[pl.ds(pl.multiple_of(CF + core * FL, FL), FL)],
            lsem.at[5],
        ),
    ]
    for copy in loads:
        copy.start()

    qrow = lax.broadcasted_iota(jnp.int32, (NQ, R), 0)
    qcol = lax.broadcasted_iota(jnp.int32, (NQ, R), 1)
    qg = lax.shift_right_logical(qrow, 4)
    qk = lax.bitwise_and(qrow, KP - 1)

    def by_expert(el):
        return ones_where((qcol == qg * (2 * SL) + el * SL + qk) & (qk < SL))

    def by_half(half):
        return ones_where((qcol == half * HR + qg * SL + qk) & (qk < SL))

    acc[...] = jnp.zeros_like(acc)
    for c in range(2):
        bh[c] = by_half(c)
    for copy in loads[:3]:
        copy.wait()
    tok_of = lax.broadcasted_iota(jnp.int32, (R, R), 0)
    ot[...] = ones_where(tok_of == rt[...])
    ordered = dot(both[...], ot[...], NN).astype(BF)
    pad = jnp.zeros((NQ, 64), BF)
    for el in range(2):
        block = dot(by_expert(el), ordered, NT).astype(BF)
        sbuf[el] = jnp.concatenate([block, pad], axis=1).reshape(NE, KP, CH + 64)
    pl.semaphore_wait(barrier, len(peers))

    for rel, o in sorted(pairs, key=lambda p: -min(p[1], NE - p[1])):
        to = core if rel == 0 else other
        k = rel * NE + o
        go(sbuf.at[to, ea(o)], rbuf.at[core, e], a_s.at[k], a_r.at[k], (ea(o), tid(x, y, to)))
    rbuf[core, e] = sbuf[core, e]
    mine = pl.ds(pl.multiple_of(core * FL, FL), FL)
    mine_dn = pl.ds(pl.multiple_of(CF + core * FL, FL), FL)
    his = pl.ds(pl.multiple_of(other * FL, FL), FL)
    his_dn = pl.ds(pl.multiple_of(CF + other * FL, FL), FL)
    go(up_hbm.at[his], w.at[mine], w_s.at[0], w_r.at[0], sib)
    go(down_hbm.at[his], w.at[mine_dn], w_s.at[1], w_r.at[1], sib)
    for rel, o in pairs:
        k = rel * NE + o
        got(rbuf.at[core if rel == 0 else other, ea(-o)], a_s.at[k], a_r.at[k])
    for c in range(2):
        landed = rbuf[c].reshape(NQ, CH + 64)
        part = dot(landed[:, :CW], bh[0], TN) + dot(landed[:, CW:CH], bh[1], TN)
        xg[pl.ds(pl.multiple_of(chip * CH + c * CW, CW), CW), :] = part.astype(BF)

    def chunk(xx, yy):
        return xg.at[pl.ds(pl.multiple_of((xx * Y + yy) * CH, CH), CH)]

    order = [0] + sorted(range(1, Y), key=lambda d: min(d, Y - d))
    halves = (set(range(Y // 2)), set(range(Y // 2, Y)))

    def slot(direction, step, j):
        return (direction * (H + 1) + step) * Y + j

    def onward(direction, step, j, piece):
        to = (e, tid(xa(1 if direction == 0 else -1), y, core))
        k = slot(direction, step, j)
        go(piece, piece, ring_s.at[k], ring_r.at[k], to)

    own = chunk(x, y)
    onward(0, 1, 0, own)
    onward(1, 1, 0, own)
    for dy in reversed(order[1:]):
        go(own, own, y_s.at[dy], y_r.at[dy], (e, tid(x, ya(dy), core)))

    drain()
    for copy in loads[3:]:
        copy.wait()
    got(w.at[his], w_s.at[0], w_r.at[0])
    got(w.at[his_dn], w_s.at[1], w_r.at[1])
    erow = lax.broadcasted_iota(jnp.int32, (KP, D), 0)
    both_emb = emb[...].astype(F32)
    own_emb = jnp.where(core == 0, both_emb[0:1], both_emb[1:2])
    w[pl.ds(2 * CF, KP), :] = jnp.where(erow == 0, own_emb, 0.0).astype(BF)

    def spread(xx):
        at = pl.ds(xx * SW, SW)
        srow = lax.broadcasted_iota(jnp.int32, (SW, PW), 0)
        scol = lax.broadcasted_iota(jnp.int32, (SW, PW), 1)
        src = (scol // CW) * CH + lax.rem(scol, CW)
        for c in range(2):
            pick = ones_where(srow == src + c * CW)
            u2[pl.ds(c * CF, CF), pl.ds(xx * PW, PW)] = dot(w[pl.ds(0, CF), at], pick, NN).astype(BF)

    def use(xx):
        at = pl.ds(pl.multiple_of(xx * SW, SW), SW)
        acc[...] += dot(w[:, at], xg[at, :], NN)

    for j, dy in enumerate(order):
        if dy:
            piece = chunk(x, ya(-dy))
            got(piece, y_s.at[dy], y_r.at[dy])
            onward(0, 1, j, piece)
            onward(1, 1, j, piece)
    use(x)
    for step in range(1, H + 1):
        for j, dy in enumerate(order):
            for direction in range(2):
                if step == H and j not in halves[direction]:
                    continue
                piece = chunk(xa(-step if direction == 0 else step), ya(-dy))
                k = slot(direction, step, j)
                got(piece, ring_s.at[k], ring_r.at[k])
                if step < H - 1 or (step == H - 1 and j in halves[direction]):
                    onward(direction, step + 1, j, piece)
        if step < H:
            use(xa(-step))
            use(xa(step))
            for k in range((step - 1) * X // (H - 1), step * X // (H - 1)):
                spread(k)
    use(xa(H))

    lane = lax.broadcasted_iota(jnp.int32, (1, R), 1)
    lo = lane < HR

    def doubled(v, half):
        turned = pltpu.roll(v, HR, 1)
        return jnp.where(lo, v, turned) if half == 0 else jnp.where(lo, turned, v)

    hidden = doubled(acc[pl.ds(0, CF), :], 0)
    back = doubled(acc[pl.ds(CF, CF), :], 1)
    logit = doubled(acc[pl.ds(2 * CF, 8), :], 0)[0:1]
    gating = 1.0 / (1.0 + jnp.exp(-logit))
    c0 = 0.7978845608028654
    c1 = 0.044715
    sq = hidden * hidden
    th = jnp.tanh(c0 * (hidden + c1 * (sq * hidden)))
    cdf = 0.5 * (1.0 + th)
    act = hidden * cdf
    slope = cdf + (0.5 * hidden) * (1.0 - th * th) * (c0 * (1.0 + (3.0 * c1) * sq))
    zero = jnp.zeros_like(hidden)
    pre = slope * (gating * back)
    pre_lo = jnp.where(lo, pre, zero).astype(BF)
    bd[pl.ds(0, CF), :] = pre_lo
    bd[pl.ds(CF, CF), :] = jnp.where(lo, zero, pre).astype(BF)

    def partial(d):
        xx = xa(d)
        at = pl.ds(pl.multiple_of(xx * PW, PW), PW)
        pf[xx] = dot(u2[:, at], bd[...], TN).reshape(Y, CW, R)

    ahead = sorted(range(Y), key=lambda d: -min(d, Y - d))

    def pass_on(direction, m, j):
        to = (e, tid(xa(1 if direction == 0 else -1), y, core))
        k = slot(direction, m, j)
        go(outb.at[direction, m, j], inb.at[direction, m, j], ch_s.at[k], ch_r.at[k], to)

    def came(direction, m, j):
        k = slot(direction, m, j)
        got(inb.at[direction, m, j], ch_s.at[k], ch_r.at[k])
        return inb[direction, m, j].astype(F32)

    partial(H)
    for j in range(Y):
        direction = 0 if j in halves[0] else 1
        outb[direction, 1, j] = pf[xa(H), ya(ahead[j])].astype(BF)
        pass_on(direction, 1, j)

    l2[pl.ds(0, CF), :] = pre_lo
    l2[pl.ds(CF, CF), :] = jnp.where(lo, zero, act * gating).astype(BF)
    gp[...] = jnp.sum(act.astype(BF).astype(F32) * back, axis=0, keepdims=True)
    for dy in range(1, Y):
        go(gp, gy.at[dy], gy_s.at[dy], gy_r.at[dy], (e, tid(x, ya(dy), core)))
    def grads(k):
        at = pl.ds(k * SW, SW)
        gr[:, at] = dot(l2[...], xg[at, :], NT).astype(BF)

    done = 0
    for m in range(2, H + 1):
        if m == 2:
            partial(H - 1)
            partial(1 - H)
        for first_part in (True, False):
            if m == 2 and not first_part:
                for d in range(H - 2, 0, -1):
                    partial(d)
                    partial(-d)
                partial(0)
            for j in range(Y):
                for direction in range(2):
                    late = j in halves[direction]
                    if late == first_part:
                        continue
                    dest = xa((H + 1 - m) * (1 if direction == 0 else -1))
                    value = pf[dest, ya(ahead[j])]
                    if m > 2 or late:
                        value = value + came(direction, m - 1, j)
                    outb[direction, m, j] = value.astype(BF)
                    pass_on(direction, m, j)
        drain()
        if m == 2:
            total = gp[...]
            for dy in range(1, Y):
                got(gy.at[dy], gy_s.at[dy], gy_r.at[dy])
                total = total + gy[dy]
            gs[...] = total
            for dx in range(1, X):
                go(gs, gx.at[dx], gx_s.at[dx], gx_r.at[dx], (e, tid(xa(dx), y, core)))
        for _ in range(X // (H - 1)):
            grads(done)
            done += 1
    while done < X:
        grads(done)
        done += 1
    outs = [
        pltpu.make_async_copy(gr.at[mine], ug_hbm.at[mine], osem.at[0]),
        pltpu.make_async_copy(gr.at[mine_dn], dg_hbm.at[mine], osem.at[1]),
    ]
    for copy in outs:
        copy.start()
    go(gr.at[his], ug_hbm.at[mine], g_s.at[0], g_r.at[0], sib)
    go(gr.at[his_dn], dg_hbm.at[mine], g_s.at[1], g_r.at[1], sib)

    gate_total = gs[...]
    for dx in range(1, X):
        got(gx.at[dx], gx_s.at[dx], gx_r.at[dx])
        gate_total = gate_total + gx[dx]
    slopes = gate_total * gating * (1.0 - gating)
    srow = lax.broadcasted_iota(jnp.int32, (KP, R), 0)
    one_row = jnp.where((srow == 0) & lo, slopes, 0.0)
    hi = one_row.astype(BF)
    rest = one_row - hi.astype(F32)
    mid = rest.astype(BF)
    low = (rest - mid.astype(F32)).astype(BF)

    def embed_part(tt):
        xs = xg[pl.ds(pl.multiple_of(tt * CW, CW), CW), :]
        return (dot(hi, xs, NT) + dot(mid, xs, NT) + dot(low, xs, NT))[0:8]

    ego[...] = jnp.concatenate(
        [embed_part(tid(x, y, other)), jnp.zeros((8, 128 - CW), F32)], axis=1
    )
    go(ego, egi, e_s.at[0], e_r.at[0], sib)
    own_part = embed_part(t)[0:1]
    prow = lax.broadcasted_iota(jnp.int32, (CW, D), 0)
    pcol = lax.broadcasted_iota(jnp.int32, (CW, D), 1)
    erows = w[pl.ds(2 * CF, KP), :]
    ecol = [
        dot(ones_where(pcol == prow + (chip * CH + c * CW)), erows, NT)[:, 0:1] for c in range(2)
    ]
    outer = jnp.where(lo, ecol[0], ecol[1]) * slopes
    for el in range(2):
        otq[el] = dot(by_expert(el), ot[...], NT).astype(BF)

    for j in range(Y):
        dy = ahead[j]
        value = pf[x, ya(dy)] + came(0, H, j) + came(1, H, j)
        if dy:
            yo[dy] = value.astype(BF)
            go(yo.at[dy], yi.at[dy], yr_s.at[dy], yr_r.at[dy], (e, tid(x, ya(dy), core)))
        else:
            summed = value + outer
    drain()
    for dy in sorted(range(1, Y), key=lambda d: min(d, Y - d)):
        got(yi.at[dy], yr_s.at[dy], yr_r.at[dy])
        summed = summed + yi[dy].astype(F32)
    summed = summed.astype(BF)

    pad = jnp.zeros((NQ, 128 - CW), BF)
    for c in range(2):
        block = dot(bh[c], summed, NT).astype(BF)
        sbuf2[c] = jnp.concatenate([block, pad], axis=1).reshape(NE, KP, 128)
    for rel, o in sorted(pairs, key=lambda p: -min(p[1], NE - p[1])):
        to = core if rel == 0 else other
        k = rel * NE + o
        go(sbuf2.at[to, ea(o)], rbuf2.at[core, e], b_s.at[k], b_r.at[k], (ea(o), tid(x, y, to)))
    rbuf2[core, e] = sbuf2[core, e]
    drain()
    got(egi, e_s.at[0], e_r.at[0])
    row2 = lax.broadcasted_iota(jnp.int32, (2, CW), 0)
    egv[...] = jnp.where(row2 == core, own_part, egi[...][0:1, :CW])
    outs.append(pltpu.make_async_copy(egv, eg_hbm, osem.at[2]))
    outs[-1].start()
    got(ug_hbm.at[his], g_s.at[0], g_r.at[0])
    got(dg_hbm.at[his], g_s.at[1], g_r.at[1])
    for rel, o in pairs:
        k = rel * NE + o
        got(rbuf2.at[core if rel == 0 else other, ea(-o)], b_s.at[k], b_r.at[k])
    placed = sum(dot(rbuf2[el].reshape(NQ, 128)[:, :CW], otq[el], TN) for el in range(2))
    tgv[...] = (both[pl.ds(CW, CW), :].astype(F32) + placed).astype(BF)
    outs.append(pltpu.make_async_copy(tgv, tg_hbm, osem.at[3]))
    outs[-1].start()
    for copy in outs:
        copy.wait()


def hand_over(*refs):
    ins, outs, held, sems = refs[:4], refs[4:8], refs[8:12], refs[12]
    first = [pltpu.make_async_copy(ins[i], held[i], sems.at[i]) for i in range(4)]
    second = [pltpu.make_async_copy(held[i], outs[i], sems.at[4 + i]) for i in range(4)]
    for copy in first:
        copy.start()
    for i in range(4):
        first[i].wait()
        second[i].start()
    for copy in second:
        copy.wait()


def local(groups, tensors, tokens, cotangent, routing, up_weight, down_weight, expert_embed):
    rows, cw = tokens.shape
    el, depth, fl = up_weight.shape
    sl = rows // (groups * el)
    xs = tensors // (2 * Y)
    dims = (groups, sl, cw, xs, fl)
    h = xs // 2
    cf = 2 * fl
    vm = pltpu.VMEM
    dma = pltpu.SemaphoreType.DMA
    n_ring = 2 * (h + 1) * Y

    def pair(n):
        return [dma((n,)), dma((n,))]

    scratch = [
        vm((2 * cw, rows), BF),
        vm((1, rows), jnp.int32),
        vm((el, depth), BF),
        vm((rows, rows), BF),
        vm((2, groups * KP, rows), BF),
        vm((2, groups * KP, rows), BF),
        vm((2, groups, KP, 2 * cw + 64), BF),
        vm((2, groups, KP, 2 * cw + 64), BF),
        vm((depth, rows), BF),
        vm((2 * cf + KP, depth), BF),
        vm((2 * cf, depth // 2), BF),
        vm((2 * cf + KP, rows), F32),
        vm((2 * cf, rows), BF),
        vm((2 * cf, rows), BF),
        vm((2 * cf, depth), BF),
        vm((xs, Y, cw, rows), F32),
        vm((2, h + 1, Y, cw, rows), BF),
        vm((2, h + 1, Y, cw, rows), BF),
        vm((Y, cw, rows), F32),
        vm((Y, cw, rows), BF),
        vm((Y, cw, rows), BF),
        vm((1, rows), F32),
        vm((Y, 1, rows), F32),
        vm((1, rows), F32),
        vm((xs, 1, rows), F32),
        vm((8, 128), F32),
        vm((8, 128), F32),
        vm((el, cw), F32),
        vm((cw, rows), BF),
        vm((2, groups, KP, 128), BF),
        vm((2, groups, KP, 128), BF),
        dma((6,)),
        dma((4,)),
        *pair(2),
        *pair(2 * groups),
        *pair(Y),
        *pair(n_ring),
        *pair(n_ring),
        *pair(Y),
        *pair(Y),
        *pair(xs),
        *pair(2),
        *pair(1),
        *pair(2 * groups),
    ]
    hbm = pl.BlockSpec(memory_space=pl.ANY)
    shapes = (
        jax.ShapeDtypeStruct((cw, rows), BF),
        jax.ShapeDtypeStruct((el * fl, depth), BF),
        jax.ShapeDtypeStruct((el * fl, depth), BF),
        jax.ShapeDtypeStruct((el, cw), F32),
    )
    made = pl.pallas_call(
        functools.partial(kernel, dims),
        out_shape=shapes,
        in_specs=[hbm] * 6,
        out_specs=(hbm,) * 4,
        scratch_shapes=scratch,
        compiler_params=pltpu.CompilerParams(
            collective_id=0, has_side_effects=True, vmem_limit_bytes=60 * 1024 * 1024
        ),
    )(
        tokens.T,
        cotangent.T,
        routing,
        up_weight.transpose(0, 2, 1).reshape(el * fl, depth),
        down_weight.reshape(el * fl, depth),
        expert_embed,
    )
    tg, ug, dg, eg = pl.pallas_call(
        hand_over,
        out_shape=shapes,
        in_specs=[hbm] * 4,
        out_specs=(hbm,) * 4,
        scratch_shapes=[vm(shape.shape, shape.dtype) for shape in shapes] + [dma((8,))],
        compiler_params=pltpu.CompilerParams(vmem_limit_bytes=60 * 1024 * 1024),
    )(*made)
    return (
        tg.T,
        ug.reshape(el, fl, depth).transpose(0, 2, 1),
        dg.reshape(el, fl, depth),
        eg,
    )


def solution(mesh):
    return jax.shard_map(
        functools.partial(local, mesh.shape["expert"], mesh.shape["tensor"]),
        mesh=mesh,
        in_specs=(
            P("expert", "tensor"),
            P("expert", "tensor"),
            P("expert", None),
            P("expert", None, "tensor"),
            P("expert", "tensor", None),
            P("expert", None),
        ),
        out_specs=(
            P("expert", "tensor"),
            P("expert", None, "tensor"),
            P("expert", "tensor", None),
            P("expert", "tensor"),
        ),
        check_vma=False,
    )
```

time: 553 us -> 85.6 us (0.15)
  waiting for transfers between devices: 327 us -> 0 us
  blocking collectives: 174 us -> 0 us
  Pallas kernels: 0 us -> 84.8 us
  between operations: 14 us -> 0.64 us
  matrix products: 11 us -> 0 us
  local copies, waits for them, and re-layouts: 10.7 us -> 0 us
  starting transfers between devices: 8.11 us -> 0 us
    all_gather x2 -> x0, waiting for transfers between devices: 167 us -> none  [the longest x1 90.7 us: local(): lax.all_gather(share_g, 'tensor', axis=2, tiled=True)]
    reduce_scatter x1 -> x0, waiting for transfers between devices: 153 us -> none  [local(): lax.psum_scatter(hidden_terms, 'tensor', scatter_dimension=2, tiled=True)]
    psum x1 -> x0, blocking collectives: 139 us -> none  [local(): gate_total = lax.psum(gate_part, 'tensor')]
    pallas_call x0 -> x2, Pallas kernels: none -> 84.8 us  [the longest x1 82.7 us: local(): pl.pallas_call(functools.partial(kernel, dims), out_shape=shapes, in_spec...]
    all_to_all x2 -> x0, blocking collectives: 35.7 us -> none  [the longest x1 25.7 us: local(): lax.all_to_all(sorted_x, 'expert', split_axis=0, concat_axis=0, tiled=True)]
    dot_general x6 -> x0, matrix products: 11 us -> none  [the longest x1 2.71 us: local(): jnp.einsum('erd,efd->erf', upstream, down_weight, preferred_element_type=...]
    all_to_all x1 -> x0, starting transfers between devices: 7.98 us -> none  [local(): lax.all_to_all(outgoing, 'expert', split_axis=0, concat_axis=0, tiled=True)]
    all_to_all x1 -> x0, waiting for transfers between devices: 6.74 us -> none  [local(): lax.all_to_all(outgoing, 'expert', split_axis=0, concat_axis=0, tiled=True)]
  transfers between devices with their start and end apart: 4 -> 0, of which waited for: 4 -> 0; matrix products, arithmetic and copies ran while one was open for 1% -> 0% of each run, Pallas kernels for 0% -> 0%
where the time goes in v1:
time: 85.6 us; the launch traced here: 85.5 us
  Pallas kernels  84.8 us (99%)
    pallas_call x1, Pallas kernels, local(): pl.pallas_call(functools.partial(kernel, dims), out_shape=shapes, in_spec...  82.7 us
    pallas_call x1, Pallas kernels, local(): pl.pallas_call(hand_over, out_shape=shapes, in_specs=[hbm] * 4, out_specs...  2.1 us

profile of v1, /device:TPU:1, one launch (start us, length us, event | category | flops | bytes accessed | tf_op | source)
XLA Modules:
  0.0 85.5 jit_solution(684080900735464536)
XLA Ops:
  0.6 82.7 %shard_map.93 = (bf16[32,384]{1,0:T(8,128)(2,1)}, bf16[128,2048]{1,0:T(8,128)(2,1)}, bf16[128,2048]{1,0:T(8,128)(2,1)}, f32[2,32]{1,0:T(2,128)}) custom-call(bf16[32,384]{1,0:T(8,128)(2,1)} %bitcast.13, bf16[32,384]{1,0:T(8,128)(2,1)} %bitcast.14, s32[1,384]{1,0:T(1,128)} %rt_hbm.1, bf16[128,2048]{1,0:T(8,128)(2,1)} %bitcast.11, bf16[128,2048]{1,0:T(8,128)(2,1)} %bitcast.12, ...), custom_call_target="tpu_custom_call" | custom-call | tf_op jit(solution)/shard_map/pallas_call | solution.py:488
  83.4 2.1 %shard_map.94 = (bf16[32,384]{1,0:T(8,128)(2,1)}, bf16[128,2048]{1,0:T(8,128)(2,1)}, bf16[128,2048]{1,0:T(8,128)(2,1)}, f32[2,32]{1,0:T(2,128)}) custom-call(bf16[32,384]{1,0:T(8,128)(2,1)} %get-tuple-element.12.refs_0_, bf16[128,2048]{1,0:T(8,128)(2,1)} %get-tuple-element.13.refs_1_, bf16[128,2048]{1,0:T(8,128)(2,1)} %get-tuple-element.14.refs_2_, ...), custom_call_target="tpu_custom_call" | custom-call | tf_op jit(solution)/shard_map/pallas_call | solution.py:505

commit v2 on v1

--- a/solution.py
+++ b/solution.py
@@ -40,7 +40,7 @@
     tok_hbm, cot_hbm, rt_hbm, up_hbm, down_hbm, emb_hbm,
     tg_hbm, ug_hbm, dg_hbm, eg_hbm,
     both, rt, emb, ot, otq, bh, sbuf, rbuf, xg, w, u2, acc, l2, bd, gr,
-    pf, outb, inb, vf, yo, yi, gp, gy, gs, gx, ego, egi, egv, tgv, sbuf2, rbuf2,
+    pf, outb, inb, yo, yi, gp, gy, gs, gx, ego, egi, egv, tgv, sbuf2, rbuf2,
     lsem, osem,
     w_s, w_r, a_s, a_r, y_s, y_r, ring_s, ring_r, ch_s, ch_r, yr_s, yr_r,
     gy_s, gy_r, gx_s, gx_r, g_s, g_r, e_s, e_r, b_s, b_r,
@@ -78,10 +78,14 @@
     sib = (e, tid(x, y, other))
     sends = []
 
-    def go(src, dst, ssem, rsem, device):
+    def go(src, dst, ssem, rsem, device, single=True):
         copy = remote(src, dst, ssem, rsem, device)
         copy.start()
-        sends.append(copy)
+        if single:
+            sends.append(copy)
+
+    def gone(src, ssem, rsem):
+        remote(src, src, ssem, rsem, sib).wait_send()
 
     def drain():
         for copy in sends:
@@ -93,12 +97,10 @@
 
     barrier = pltpu.get_barrier_semaphore()
     pairs = [(rel, o) for o in range(NE) for rel in range(2) if rel or o]
+    pairs.sort(key=lambda p: -min(p[1], NE - p[1]))
     peers = [(ea(o), tid(x, y, core if rel == 0 else other)) for rel, o in pairs]
     peers += [(e, tid(x, ya(dy), core)) for dy in range(1, Y)]
     peers += [(e, tid(xa(dx), y, core)) for dx in range(1, X)]
-    for peer in peers:
-        pl.semaphore_signal(barrier, inc=1, device_id=peer, device_id_type=pl.DeviceIdType.MESH)
-
     loads = [
         pltpu.make_async_copy(rt_hbm, rt, lsem.at[0]),
         pltpu.make_async_copy(tok_hbm, both.at[pl.ds(0, CW)], lsem.at[1]),
@@ -115,7 +117,11 @@
             lsem.at[5],
         ),
     ]
-    for copy in loads:
+    for copy in loads[:3]:
+        copy.start()
+    for peer in peers:
+        pl.semaphore_signal(barrier, inc=1, device_id=peer, device_id_type=pl.DeviceIdType.MESH)
+    for copy in loads[3:]:
         copy.start()
 
     qrow = lax.broadcasted_iota(jnp.int32, (NQ, R), 0)
@@ -129,9 +135,6 @@
     def by_half(half):
         return ones_where((qcol == half * HR + qg * SL + qk) & (qk < SL))
 
-    acc[...] = jnp.zeros_like(acc)
-    for c in range(2):
-        bh[c] = by_half(c)
     for copy in loads[:3]:
         copy.wait()
     tok_of = lax.broadcasted_iota(jnp.int32, (R, R), 0)
@@ -140,32 +143,44 @@
     pad = jnp.zeros((NQ, 64), BF)
     for el in range(2):
         block = dot(by_expert(el), ordered, NT).astype(BF)
-        sbuf[el] = jnp.concatenate([block, pad], axis=1).reshape(NE, KP, CH + 64)
+        sbuf[pl.ds(el * NE, NE)] = jnp.concatenate([block, pad], axis=1).reshape(NE, KP, CH + 64)
     pl.semaphore_wait(barrier, len(peers))
 
-    for rel, o in sorted(pairs, key=lambda p: -min(p[1], NE - p[1])):
+    for rel, o in pairs:
         to = core if rel == 0 else other
-        k = rel * NE + o
-        go(sbuf.at[to, ea(o)], rbuf.at[core, e], a_s.at[k], a_r.at[k], (ea(o), tid(x, y, to)))
-    rbuf[core, e] = sbuf[core, e]
+        go(
+            sbuf.at[to * NE + ea(o)], rbuf.at[core * NE + e],
+            a_s.at[0], a_r.at[0], (ea(o), tid(x, y, to)), False,
+        )
+    rbuf[core * NE + e] = sbuf[core * NE + e]
     mine = pl.ds(pl.multiple_of(core * FL, FL), FL)
     mine_dn = pl.ds(pl.multiple_of(CF + core * FL, FL), FL)
     his = pl.ds(pl.multiple_of(other * FL, FL), FL)
     his_dn = pl.ds(pl.multiple_of(CF + other * FL, FL), FL)
     go(up_hbm.at[his], w.at[mine], w_s.at[0], w_r.at[0], sib)
     go(down_hbm.at[his], w.at[mine_dn], w_s.at[1], w_r.at[1], sib)
-    for rel, o in pairs:
-        k = rel * NE + o
-        got(rbuf.at[core if rel == 0 else other, ea(-o)], a_s.at[k], a_r.at[k])
+    acc[...] = jnp.zeros_like(acc)
     for c in range(2):
-        landed = rbuf[c].reshape(NQ, CH + 64)
+        bh[c] = by_half(c)
+    got(rbuf.at[pl.ds(0, 2 * NE - 1)], a_s.at[0], a_r.at[0])
+    for c in range(2):
+        landed = rbuf[pl.ds(c * NE, NE)].reshape(NQ, CH + 64)
         part = dot(landed[:, :CW], bh[0], TN) + dot(landed[:, CW:CH], bh[1], TN)
         xg[pl.ds(pl.multiple_of(chip * CH + c * CW, CW), CW), :] = part.astype(BF)
 
-    def chunk(xx, yy):
-        return xg.at[pl.ds(pl.multiple_of((xx * Y + yy) * CH, CH), CH)]
-
-    order = [0] + sorted(range(1, Y), key=lambda d: min(d, Y - d))
+    def chunk(xx, yy, half):
+        return xg.at[pl.ds(pl.multiple_of((xx * Y + yy) * CH + half * CW, CW), CW)]
+
+    near = sorted(range(1, Y), key=lambda d: min(d, Y - d))
+    beside = [dy for dy in near if min(dy, Y - dy) == 1]
+    beyond = [dy for dy in near if min(dy, Y - dy) > 1]
+    order = [(0, 0), (0, 1)]
+    order += [(dy, half) for group in (beside, beyond) for half in range(2) for dy in group]
+    NJ = len(order)
+
+    def gslot(direction, step, j):
+        return (direction * (H + 1) + step) * NJ + j
+
     halves = (set(range(Y // 2)), set(range(Y // 2, Y)))
 
     def slot(direction, step, j):
@@ -173,16 +188,19 @@
 
     def onward(direction, step, j, piece):
         to = (e, tid(xa(1 if direction == 0 else -1), y, core))
-        k = slot(direction, step, j)
-        go(piece, piece, ring_s.at[k], ring_r.at[k], to)
-
-    own = chunk(x, y)
-    onward(0, 1, 0, own)
-    onward(1, 1, 0, own)
-    for dy in reversed(order[1:]):
-        go(own, own, y_s.at[dy], y_r.at[dy], (e, tid(x, ya(dy), core)))
+        k = gslot(direction, step, j)
+        go(piece, piece, ring_s.at[0], ring_r.at[k], to, False)
+
+    for j in range(2):
+        for direction in range(2):
+            onward(direction, 1, j, chunk(x, y, j))
+    for dy, half in order[2:]:
+        own = chunk(x, y, half)
+        k = dy * 2 + half
+        go(own, own, y_s.at[k], y_r.at[k], (e, tid(x, ya(dy), core)))
 
     drain()
+    gone(sbuf.at[pl.ds(0, 2 * NE - 1)], a_s.at[0], a_r.at[0])
     for copy in loads[3:]:
         copy.wait()
     got(w.at[his], w_s.at[0], w_r.at[0])
@@ -205,23 +223,36 @@
         at = pl.ds(pl.multiple_of(xx * SW, SW), SW)
         acc[...] += dot(w[:, at], xg[at, :], NN)
 
-    for j, dy in enumerate(order):
-        if dy:
-            piece = chunk(x, ya(-dy))
-            got(piece, y_s.at[dy], y_r.at[dy])
-            onward(0, 1, j, piece)
-            onward(1, 1, j, piece)
+    def relay(step, j):
+        dy, half = order[j]
+        for direction in range(2):
+            if step == H and half != direction:
+                continue
+            piece = chunk(xa(-step if direction == 0 else step), ya(-dy), half)
+            got(piece, ring_s.at[0], ring_r.at[gslot(direction, step, j)])
+            if step < H - 1 or (step == H - 1 and half == direction):
+                onward(direction, step + 1, j, piece)
+
+    def beginning(j):
+        dy, half = order[j]
+        piece = chunk(x, ya(-dy), half)
+        k = dy * 2 + half
+        got(piece, y_s.at[k], y_r.at[k])
+        onward(0, 1, j, piece)
+        onward(1, 1, j, piece)
+
+    lead = 2 + len(beside)
+    for j in range(2, lead):
+        beginning(j)
+    relay(1, 0)
+    relay(1, 1)
+    for j in range(lead, NJ):
+        beginning(j)
     use(x)
     for step in range(1, H + 1):
-        for j, dy in enumerate(order):
-            for direction in range(2):
-                if step == H and j not in halves[direction]:
-                    continue
-                piece = chunk(xa(-step if direction == 0 else step), ya(-dy))
-                k = slot(direction, step, j)
-                got(piece, ring_s.at[k], ring_r.at[k])
-                if step < H - 1 or (step == H - 1 and j in halves[direction]):
-                    onward(direction, step + 1, j, piece)
+        for j in range(NJ):
+            if step > 1 or j > 1:
+                relay(step, j)
         if step < H:
             use(xa(-step))
             use(xa(step))
@@ -263,17 +294,17 @@
     def pass_on(direction, m, j):
         to = (e, tid(xa(1 if direction == 0 else -1), y, core))
         k = slot(direction, m, j)
-        go(outb.at[direction, m, j], inb.at[direction, m, j], ch_s.at[k], ch_r.at[k], to)
+        go(outb.at[k], inb.at[k], ch_s.at[0], ch_r.at[k], to, False)
 
     def came(direction, m, j):
         k = slot(direction, m, j)
-        got(inb.at[direction, m, j], ch_s.at[k], ch_r.at[k])
-        return inb[direction, m, j].astype(F32)
+        got(inb.at[k], ch_s.at[0], ch_r.at[k])
+        return inb[k].astype(F32)
 
     partial(H)
     for j in range(Y):
         direction = 0 if j in halves[0] else 1
-        outb[direction, 1, j] = pf[xa(H), ya(ahead[j])].astype(BF)
+        outb[slot(direction, 1, j)] = pf[xa(H), ya(ahead[j])].astype(BF)
         pass_on(direction, 1, j)
 
     l2[pl.ds(0, CF), :] = pre_lo
@@ -305,9 +336,8 @@
                     value = pf[dest, ya(ahead[j])]
                     if m > 2 or late:
                         value = value + came(direction, m - 1, j)
-                    outb[direction, m, j] = value.astype(BF)
+                    outb[slot(direction, m, j)] = value.astype(BF)
                     pass_on(direction, m, j)
-        drain()
         if m == 2:
             total = gp[...]
             for dy in range(1, Y):
@@ -370,7 +400,9 @@
             go(yo.at[dy], yi.at[dy], yr_s.at[dy], yr_r.at[dy], (e, tid(x, ya(dy), core)))
         else:
             summed = value + outer
-    drain()
+    n_half = (2 * H - 1) * Y
+    gone(xg.at[pl.ds(0, n_half * CH)], ring_s.at[0], ring_r.at[0])
+    gone(outb.at[pl.ds(0, n_half)], ch_s.at[0], ch_r.at[0])
     for dy in sorted(range(1, Y), key=lambda d: min(d, Y - d)):
         got(yi.at[dy], yr_s.at[dy], yr_r.at[dy])
         summed = summed + yi[dy].astype(F32)
@@ -379,12 +411,14 @@
     pad = jnp.zeros((NQ, 128 - CW), BF)
     for c in range(2):
         block = dot(bh[c], summed, NT).astype(BF)
-        sbuf2[c] = jnp.concatenate([block, pad], axis=1).reshape(NE, KP, 128)
-    for rel, o in sorted(pairs, key=lambda p: -min(p[1], NE - p[1])):
+        sbuf2[pl.ds(c * NE, NE)] = jnp.concatenate([block, pad], axis=1).reshape(NE, KP, 128)
+    for rel, o in pairs:
         to = core if rel == 0 else other
-        k = rel * NE + o
-        go(sbuf2.at[to, ea(o)], rbuf2.at[core, e], b_s.at[k], b_r.at[k], (ea(o), tid(x, y, to)))
-    rbuf2[core, e] = sbuf2[core, e]
+        go(
+            sbuf2.at[to * NE + ea(o)], rbuf2.at[core * NE + e],
+            b_s.at[0], b_r.at[0], (ea(o), tid(x, y, to)), False,
+        )
+    rbuf2[core * NE + e] = sbuf2[core * NE + e]
     drain()
     got(egi, e_s.at[0], e_r.at[0])
     row2 = lax.broadcasted_iota(jnp.int32, (2, CW), 0)
@@ -393,10 +427,11 @@
     outs[-1].start()
     got(ug_hbm.at[his], g_s.at[0], g_r.at[0])
     got(dg_hbm.at[his], g_s.at[1], g_r.at[1])
-    for rel, o in pairs:
-        k = rel * NE + o
-        got(rbuf2.at[core if rel == 0 else other, ea(-o)], b_s.at[k], b_r.at[k])
-    placed = sum(dot(rbuf2[el].reshape(NQ, 128)[:, :CW], otq[el], TN) for el in range(2))
+    gone(sbuf2.at[pl.ds(0, 2 * NE - 1)], b_s.at[0], b_r.at[0])
+    got(rbuf2.at[pl.ds(0, 2 * NE - 1)], b_s.at[0], b_r.at[0])
+    placed = sum(
+        dot(rbuf2[pl.ds(el * NE, NE)].reshape(NQ, 128)[:, :CW], otq[el], TN) for el in range(2)
+    )
     tgv[...] = (both[pl.ds(CW, CW), :].astype(F32) + placed).astype(BF)
     outs.append(pltpu.make_async_copy(tgv, tg_hbm, osem.at[3]))
     outs[-1].start()
@@ -439,8 +474,8 @@
         vm((rows, rows), BF),
         vm((2, groups * KP, rows), BF),
         vm((2, groups * KP, rows), BF),
-        vm((2, groups, KP, 2 * cw + 64), BF),
-        vm((2, groups, KP, 2 * cw + 64), BF),
+        vm((2 * groups, KP, 2 * cw + 64), BF),
+        vm((2 * groups, KP, 2 * cw + 64), BF),
         vm((depth, rows), BF),
         vm((2 * cf + KP, depth), BF),
         vm((2 * cf, depth // 2), BF),
@@ -449,9 +484,8 @@
         vm((2 * cf, rows), BF),
         vm((2 * cf, depth), BF),
         vm((xs, Y, cw, rows), F32),
-        vm((2, h + 1, Y, cw, rows), BF),
-        vm((2, h + 1, Y, cw, rows), BF),
-        vm((Y, cw, rows), F32),
+        vm((2 * (h + 1) * Y, cw, rows), BF),
+        vm((2 * (h + 1) * Y, cw, rows), BF),
         vm((Y, cw, rows), BF),
         vm((Y, cw, rows), BF),
         vm((1, rows), F32),
@@ -462,21 +496,21 @@
         vm((8, 128), F32),
         vm((el, cw), F32),
         vm((cw, rows), BF),
-        vm((2, groups, KP, 128), BF),
-        vm((2, groups, KP, 128), BF),
+        vm((2 * groups, KP, 128), BF),
+        vm((2 * groups, KP, 128), BF),
         dma((6,)),
         dma((4,)),
         *pair(2),
-        *pair(2 * groups),
-        *pair(Y),
-        *pair(n_ring),
-        *pair(n_ring),
+        *pair(1),
+        *pair(2 * Y),
+        dma((1,)), dma((2 * n_ring,)),
+        dma((1,)), dma((n_ring,)),
         *pair(Y),
         *pair(Y),
         *pair(xs),
         *pair(2),
         *pair(1),
-        *pair(2 * groups),
+        *pair(1),
     ]
     hbm = pl.BlockSpec(memory_space=pl.ANY)
     shapes = (

time: 85.6 us -> 81 us (0.946)
  Pallas kernels: 84.8 us -> 80.1 us
    pallas_call x1, Pallas kernels: 82.7 us -> 78 us  [local(): pl.pallas_call(functools.partial(kernel, dims), out_shape=shapes, in_spec...]
where the time goes in v2:
time: 81 us; the launch traced here: 80.8 us
  Pallas kernels  80.1 us (99%)
    pallas_call x1, Pallas kernels, local(): pl.pallas_call(functools.partial(kernel, dims), out_shape=shapes, in_spec...  78 us
    pallas_call x1, Pallas kernels, local(): pl.pallas_call(hand_over, out_shape=shapes, in_specs=[hbm] * 4, out_specs...  2.1 us

profile of v2, /device:TPU:1, one launch (start us, length us, event | category | flops | bytes accessed | tf_op | source)
XLA Modules:
  0.0 80.8 jit_solution(16130511268934740302)
XLA Ops:
  0.6 78.0 %shard_map.93 = (bf16[32,384]{1,0:T(8,128)(2,1)}, bf16[128,2048]{1,0:T(8,128)(2,1)}, bf16[128,2048]{1,0:T(8,128)(2,1)}, f32[2,32]{1,0:T(2,128)}) custom-call(bf16[32,384]{1,0:T(8,128)(2,1)} %bitcast.13, bf16[32,384]{1,0:T(8,128)(2,1)} %bitcast.14, s32[1,384]{1,0:T(1,128)} %rt_hbm.1, bf16[128,2048]{1,0:T(8,128)(2,1)} %bitcast.11, bf16[128,2048]{1,0:T(8,128)(2,1)} %bitcast.12, ...), custom_call_target="tpu_custom_call" | custom-call | tf_op jit(solution)/shard_map/pallas_call | solution.py:522
  78.7 2.1 %shard_map.94 = (bf16[32,384]{1,0:T(8,128)(2,1)}, bf16[128,2048]{1,0:T(8,128)(2,1)}, bf16[128,2048]{1,0:T(8,128)(2,1)}, f32[2,32]{1,0:T(2,128)}) custom-call(bf16[32,384]{1,0:T(8,128)(2,1)} %get-tuple-element.12.refs_0_, bf16[128,2048]{1,0:T(8,128)(2,1)} %get-tuple-element.13.refs_1_, bf16[128,2048]{1,0:T(8,128)(2,1)} %get-tuple-element.14.refs_2_, ...), custom_call_target="tpu_custom_call" | custom-call | tf_op jit(solution)/shard_map/pallas_call | solution.py:539

commit v3 on v2

--- a/solution.py
+++ b/solution.py
@@ -9,6 +9,7 @@
 
 Y = 4
 KP = 16
+CUT = 32
 BF = jnp.bfloat16
 F32 = jnp.float32
 NN = ((1,), (0,))
@@ -39,7 +40,7 @@
     dims,
     tok_hbm, cot_hbm, rt_hbm, up_hbm, down_hbm, emb_hbm,
     tg_hbm, ug_hbm, dg_hbm, eg_hbm,
-    both, rt, emb, ot, otq, bh, sbuf, rbuf, xg, w, u2, acc, l2, bd, gr,
+    both, rt, emb, ot, otq, bh, ec, sbuf, rbuf, xg, w, u2, acc, l2, bd, gr,
     pf, outb, inb, yo, yi, gp, gy, gs, gx, ego, egi, egv, tgv, sbuf2, rbuf2,
     lsem, osem,
     w_s, w_r, a_s, a_r, y_s, y_r, ring_s, ring_r, ch_s, ch_r, yr_s, yr_r,
@@ -162,6 +163,7 @@
     acc[...] = jnp.zeros_like(acc)
     for c in range(2):
         bh[c] = by_half(c)
+        otq[c] = dot(by_expert(c), ot[...], NT).astype(BF)
     got(rbuf.at[pl.ds(0, 2 * NE - 1)], a_s.at[0], a_r.at[0])
     for c in range(2):
         landed = rbuf[pl.ds(c * NE, NE)].reshape(NQ, CH + 64)
@@ -209,6 +211,16 @@
     both_emb = emb[...].astype(F32)
     own_emb = jnp.where(core == 0, both_emb[0:1], both_emb[1:2])
     w[pl.ds(2 * CF, KP), :] = jnp.where(erow == 0, own_emb, 0.0).astype(BF)
+
+    prow = lax.broadcasted_iota(jnp.int32, (CW, D), 0)
+    pcol = lax.broadcasted_iota(jnp.int32, (CW, D), 1)
+    erows = w[pl.ds(2 * CF, KP), :]
+    ecol = [
+        dot(ones_where(pcol == prow + (chip * CH + c * CW)), erows, NT)[:, 0:1] for c in range(2)
+    ]
+    lane = lax.broadcasted_iota(jnp.int32, (1, R), 1)
+    lo = lane < HR
+    ec[...] = jnp.where(lo, ecol[0], ecol[1])
 
     def spread(xx):
         at = pl.ds(xx * SW, SW)
@@ -260,8 +272,6 @@
                 spread(k)
     use(xa(H))
 
-    lane = lax.broadcasted_iota(jnp.int32, (1, R), 1)
-    lo = lane < HR
 
     def doubled(v, half):
         turned = pltpu.roll(v, HR, 1)
@@ -291,8 +301,8 @@
 
     ahead = sorted(range(Y), key=lambda d: -min(d, Y - d))
 
-    def pass_on(direction, m, j):
-        to = (e, tid(xa(1 if direction == 0 else -1), y, core))
+    def pass_on(direction, m, j, hops=1):
+        to = (e, tid(xa(hops if direction == 0 else -hops), y, core))
         k = slot(direction, m, j)
         go(outb.at[k], inb.at[k], ch_s.at[0], ch_r.at[k], to, False)
 
@@ -305,7 +315,7 @@
     for j in range(Y):
         direction = 0 if j in halves[0] else 1
         outb[slot(direction, 1, j)] = pf[xa(H), ya(ahead[j])].astype(BF)
-        pass_on(direction, 1, j)
+        pass_on(direction, 1, j, 2)
 
     l2[pl.ds(0, CF), :] = pre_lo
     l2[pl.ds(CF, CF), :] = jnp.where(lo, zero, act * gating).astype(BF)
@@ -321,20 +331,21 @@
         if m == 2:
             partial(H - 1)
             partial(1 - H)
-        for first_part in (True, False):
-            if m == 2 and not first_part:
-                for d in range(H - 2, 0, -1):
-                    partial(d)
-                    partial(-d)
-                partial(0)
+        if m == 3:
+            for d in range(H - 2, 0, -1):
+                partial(d)
+                partial(-d)
+            partial(0)
+        for late in (True, False):
             for j in range(Y):
                 for direction in range(2):
-                    late = j in halves[direction]
-                    if late == first_part:
+                    if (j in halves[direction]) != late:
                         continue
                     dest = xa((H + 1 - m) * (1 if direction == 0 else -1))
                     value = pf[dest, ya(ahead[j])]
-                    if m > 2 or late:
+                    if m == 3 and late:
+                        value = value + came(direction, 1, j)
+                    if m > 2:
                         value = value + came(direction, m - 1, j)
                     outb[slot(direction, m, j)] = value.astype(BF)
                     pass_on(direction, m, j)
@@ -382,16 +393,7 @@
     )
     go(ego, egi, e_s.at[0], e_r.at[0], sib)
     own_part = embed_part(t)[0:1]
-    prow = lax.broadcasted_iota(jnp.int32, (CW, D), 0)
-    pcol = lax.broadcasted_iota(jnp.int32, (CW, D), 1)
-    erows = w[pl.ds(2 * CF, KP), :]
-    ecol = [
-        dot(ones_where(pcol == prow + (chip * CH + c * CW)), erows, NT)[:, 0:1] for c in range(2)
-    ]
-    outer = jnp.where(lo, ecol[0], ecol[1]) * slopes
-    for el in range(2):
-        otq[el] = dot(by_expert(el), ot[...], NT).astype(BF)
-
+    outer = ec[...] * slopes
     for j in range(Y):
         dy = ahead[j]
         value = pf[x, ya(dy)] + came(0, H, j) + came(1, H, j)
@@ -441,13 +443,17 @@
 
 def hand_over(*refs):
     ins, outs, held, sems = refs[:4], refs[4:8], refs[8:12], refs[12]
-    first = [pltpu.make_async_copy(ins[i], held[i], sems.at[i]) for i in range(4)]
-    second = [pltpu.make_async_copy(held[i], outs[i], sems.at[4 + i]) for i in range(4)]
-    for copy in first:
-        copy.start()
-    for i in range(4):
-        first[i].wait()
-        second[i].start()
+    places = [(i, pl.ds(r, CUT)) for r in range(0, ins[1].shape[0], CUT) for i in (1, 2)]
+    places += [(0, pl.ds(0, ins[0].shape[0])), (3, pl.ds(0, ins[3].shape[0]))]
+    n = len(places)
+    first, second = [], []
+    for k, (i, at) in enumerate(places):
+        first.append(pltpu.make_async_copy(ins[i].at[at], held[i].at[at], sems.at[k]))
+        second.append(pltpu.make_async_copy(held[i].at[at], outs[i].at[at], sems.at[n + k]))
+        first[k].start()
+    for k in range(n):
+        first[k].wait()
+        second[k].start()
     for copy in second:
         copy.wait()
 
@@ -474,6 +480,7 @@
         vm((rows, rows), BF),
         vm((2, groups * KP, rows), BF),
         vm((2, groups * KP, rows), BF),
+        vm((cw, rows), F32),
         vm((2 * groups, KP, 2 * cw + 64), BF),
         vm((2 * groups, KP, 2 * cw + 64), BF),
         vm((depth, rows), BF),
@@ -541,7 +548,7 @@
         out_shape=shapes,
         in_specs=[hbm] * 4,
         out_specs=(hbm,) * 4,
-        scratch_shapes=[vm(shape.shape, shape.dtype) for shape in shapes] + [dma((8,))],
+        scratch_shapes=[vm(shape.shape, shape.dtype) for shape in shapes] + [dma((4 * (el * fl // CUT) + 4,))],
         compiler_params=pltpu.CompilerParams(vmem_limit_bytes=60 * 1024 * 1024),
     )(*made)
     return (

time: 81 us -> 80.7 us (level)
  no operation moved by 1% of the time
where the time goes in v3:
time: 80.7 us; the launch traced here: 80.5 us
  Pallas kernels  79.8 us (99%)
    pallas_call x1, Pallas kernels, local(): pl.pallas_call(functools.partial(kernel, dims), out_shape=shapes, in_spec...  77.7 us
    pallas_call x1, Pallas kernels, local(): pl.pallas_call(hand_over, out_shape=shapes, in_specs=[hbm] * 4, out_specs...  2.13 us

profile of v3, /device:TPU:1, one launch (start us, length us, event | category | flops | bytes accessed | tf_op | source)
XLA Modules:
  0.0 80.5 jit_solution(11932289265857131895)
XLA Ops:
  0.6 77.7 %shard_map.93 = (bf16[32,384]{1,0:T(8,128)(2,1)}, bf16[128,2048]{1,0:T(8,128)(2,1)}, bf16[128,2048]{1,0:T(8,128)(2,1)}, f32[2,32]{1,0:T(2,128)}) custom-call(bf16[32,384]{1,0:T(8,128)(2,1)} %bitcast.13, bf16[32,384]{1,0:T(8,128)(2,1)} %bitcast.14, s32[1,384]{1,0:T(1,128)} %rt_hbm.1, bf16[128,2048]{1,0:T(8,128)(2,1)} %bitcast.11, bf16[128,2048]{1,0:T(8,128)(2,1)} %bitcast.12, ...), custom_call_target="tpu_custom_call" | custom-call | tf_op jit(solution)/shard_map/pallas_call | solution.py:529
  78.4 2.1 %shard_map.94 = (bf16[32,384]{1,0:T(8,128)(2,1)}, bf16[128,2048]{1,0:T(8,128)(2,1)}, bf16[128,2048]{1,0:T(8,128)(2,1)}, f32[2,32]{1,0:T(2,128)}) custom-call(bf16[32,384]{1,0:T(8,128)(2,1)} %get-tuple-element.12.refs_0_, bf16[128,2048]{1,0:T(8,128)(2,1)} %get-tuple-element.13.refs_1_, bf16[128,2048]{1,0:T(8,128)(2,1)} %get-tuple-element.14.refs_2_, ...), custom_call_target="tpu_custom_call" | custom-call | tf_op jit(solution)/shard_map/pallas_call | solution.py:546

commit v4 on v3

--- a/solution.py
+++ b/solution.py
@@ -165,11 +165,6 @@
         bh[c] = by_half(c)
         otq[c] = dot(by_expert(c), ot[...], NT).astype(BF)
     got(rbuf.at[pl.ds(0, 2 * NE - 1)], a_s.at[0], a_r.at[0])
-    for c in range(2):
-        landed = rbuf[pl.ds(c * NE, NE)].reshape(NQ, CH + 64)
-        part = dot(landed[:, :CW], bh[0], TN) + dot(landed[:, CW:CH], bh[1], TN)
-        xg[pl.ds(pl.multiple_of(chip * CH + c * CW, CW), CW), :] = part.astype(BF)
-
     def chunk(xx, yy, half):
         return xg.at[pl.ds(pl.multiple_of((xx * Y + yy) * CH + half * CW, CW), CW)]
 
@@ -193,13 +188,25 @@
         k = gslot(direction, step, j)
         go(piece, piece, ring_s.at[0], ring_r.at[k], to, False)
 
-    for j in range(2):
-        for direction in range(2):
-            onward(direction, 1, j, chunk(x, y, j))
-    for dy, half in order[2:]:
+    def make_half(c):
+        landed = rbuf[pl.ds(c * NE, NE)].reshape(NQ, CH + 64)
+        part = dot(landed[:, :CW], bh[0], TN) + dot(landed[:, CW:CH], bh[1], TN)
+        xg[pl.ds(pl.multiple_of(chip * CH + c * CW, CW), CW), :] = part.astype(BF)
+
+    def to_column(dy, half):
         own = chunk(x, y, half)
         k = dy * 2 + half
         go(own, own, y_s.at[k], y_r.at[k], (e, tid(x, ya(dy), core)))
+
+    for half in range(2):
+        make_half(half)
+        for direction in range(2):
+            onward(direction, 1, half, chunk(x, y, half))
+        for dy in beside:
+            to_column(dy, half)
+    for half in range(2):
+        for dy in beyond:
+            to_column(dy, half)
 
     drain()
     gone(sbuf.at[pl.ds(0, 2 * NE - 1)], a_s.at[0], a_r.at[0])
@@ -411,15 +418,16 @@
     summed = summed.astype(BF)
 
     pad = jnp.zeros((NQ, 128 - CW), BF)
-    for c in range(2):
-        block = dot(bh[c], summed, NT).astype(BF)
-        sbuf2[pl.ds(c * NE, NE)] = jnp.concatenate([block, pad], axis=1).reshape(NE, KP, 128)
-    for rel, o in pairs:
+    for rel in (1, 0):
         to = core if rel == 0 else other
-        go(
-            sbuf2.at[to * NE + ea(o)], rbuf2.at[core * NE + e],
-            b_s.at[0], b_r.at[0], (ea(o), tid(x, y, to)), False,
-        )
+        block = dot(bh[to], summed, NT).astype(BF)
+        sbuf2[pl.ds(to * NE, NE)] = jnp.concatenate([block, pad], axis=1).reshape(NE, KP, 128)
+        for way, o in pairs:
+            if way == rel:
+                go(
+                    sbuf2.at[to * NE + ea(o)], rbuf2.at[core * NE + e],
+                    b_s.at[0], b_r.at[0], (ea(o), tid(x, y, to)), False,
+                )
     rbuf2[core * NE + e] = sbuf2[core * NE + e]
     drain()
     got(egi, e_s.at[0], e_r.at[0])

time: 80.7 us -> 80.4 us (level)
  no operation moved by 1% of the time
where the time goes in v4:
time: 80.4 us; the launch traced here: 80.2 us
  Pallas kernels  79.6 us (99%)
    pallas_call x1, Pallas kernels, local(): pl.pallas_call(functools.partial(kernel, dims), out_shape=shapes, in_spec...  77.5 us
    pallas_call x1, Pallas kernels, local(): pl.pallas_call(hand_over, out_shape=shapes, in_specs=[hbm] * 4, out_specs...  2.13 us

profile of v4, /device:TPU:1, one launch (start us, length us, event | category | flops | bytes accessed | tf_op | source)
XLA Modules:
  0.0 80.2 jit_solution(11065910178416466783)
XLA Ops:
  0.6 77.5 %shard_map.93 = (bf16[32,384]{1,0:T(8,128)(2,1)}, bf16[128,2048]{1,0:T(8,128)(2,1)}, bf16[128,2048]{1,0:T(8,128)(2,1)}, f32[2,32]{1,0:T(2,128)}) custom-call(bf16[32,384]{1,0:T(8,128)(2,1)} %bitcast.13, bf16[32,384]{1,0:T(8,128)(2,1)} %bitcast.14, s32[1,384]{1,0:T(1,128)} %rt_hbm.1, bf16[128,2048]{1,0:T(8,128)(2,1)} %bitcast.11, bf16[128,2048]{1,0:T(8,128)(2,1)} %bitcast.12, ...), custom_call_target="tpu_custom_call" | custom-call | tf_op jit(solution)/shard_map/pallas_call | solution.py:537
  78.1 2.1 %shard_map.94 = (bf16[32,384]{1,0:T(8,128)(2,1)}, bf16[128,2048]{1,0:T(8,128)(2,1)}, bf16[128,2048]{1,0:T(8,128)(2,1)}, f32[2,32]{1,0:T(2,128)}) custom-call(bf16[32,384]{1,0:T(8,128)(2,1)} %get-tuple-element.12.refs_0_, bf16[128,2048]{1,0:T(8,128)(2,1)} %get-tuple-element.13.refs_1_, bf16[128,2048]{1,0:T(8,128)(2,1)} %get-tuple-element.14.refs_2_, ...), custom_call_target="tpu_custom_call" | custom-call | tf_op jit(solution)/shard_map/pallas_call | solution.py:554
